TPU v7x, 32 devices: a whole 2x2x4 slice. The times are simulated.
32 devices in a mesh: vin: 8 (over z, core), vout: 2 (over x), cell: 2 (over y).
Axes of the slice: x: 2, y: 2, z: 4, core: 2. Of those that a mesh axis runs over, the one named last changes fastest.
Arguments:
- distribution: bfloat16 [8, 13824, 4, 128], P('vout', 'vin', 'cell'), may hold values from -6 to 6
- collision: bfloat16 [13824, 13824], P('vout', 'vin'), may hold values from -1 to 3
- speeds: float32 [3, 13824], P(None, 'vout'), may hold values from 0.05 to 0.3
- directions: int32 [3, 13824], P(None, 'vout'), may hold values from 0 to 1
- cell_flags: int32 [8, 4, 128], P('vin', 'cell'), may hold values 0 or 1
Outputs:
- updated: bfloat16 [8, 13824, 4, 128], P('vin', 'vout', 'cell')
Inputs may be any that keep to these rules, and one draw needn't show every extreme that they name: `directions`: 1 means the component is positive, 0 negative. `cell_flags`: 1 marks a solid cell, where nothing is transported.
All inputs are finite; a program needn't handle non-finite values. No bound on the sum of `cell_flags` on one device may be relied on, other than what follows from the above.
Results may differ from a plain program's by a relative error of at most 0.023.
Values may be sent and summed in bfloat16 or wider, within the bound.
A program may use at most 128 MiB of HBM per device.

v0:
```python
import jax
import jax.numpy as jnp
from jax import lax
from jax.sharding import PartitionSpec as P

CHUNKS = 3
CORES = 2


def from_lower(values, axis):
    ends = lax.axis_size(axis) - 1
    return lax.ppermute(values, axis, [(i, i + 1) for i in range(ends)])


def from_higher(values, axis):
    ends = lax.axis_size(axis) - 1
    return lax.ppermute(values, axis, [(i + 1, i) for i in range(ends)])


def hop(values, axis, pairs):
    return lax.ppermute(values, axis, pairs)


def core_pairs(axis):
    return [(i, i + 1 - 2 * (i % CORES)) for i in range(lax.axis_size(axis))]


def scatter_line(own, axis):
    chips = lax.axis_size(axis) // CORES
    chip = lax.axis_index(axis) // CORES
    total = lax.dynamic_index_in_dim(own, chip, 0, keepdims=False).astype(jnp.float32)
    up = down = None
    for step in range(chips - 1):
        target = jnp.clip(chips - 1 - step + chip, 0, chips - 1)
        lower = jnp.clip(step - (chips - 1 - chip), 0, chips - 1)
        send_up = lax.dynamic_index_in_dim(own, target, 0, keepdims=False)
        send_down = lax.dynamic_index_in_dim(own, lower, 0, keepdims=False)
        if step:
            send_up = (send_up.astype(jnp.float32) + up.astype(jnp.float32)).astype(own.dtype)
            send_down = (send_down.astype(jnp.float32) + down.astype(jnp.float32)).astype(own.dtype)
        rising, falling = ([], [])
        for at in range(step + 1):
            mirror = chips - 1 - at
            for core in range(CORES):
                rising.append((at * CORES + core, (at + 1) * CORES + core))
                falling.append((mirror * CORES + core, (mirror - 1) * CORES + core))
        up = hop(send_up, axis, rising)
        down = hop(send_down, axis, falling)
    if up is not None:
        total = total + up.astype(jnp.float32) + down.astype(jnp.float32)
    return total.astype(own.dtype)


def shifted(values, step):
    edge = jnp.zeros_like(values[..., :1])
    if step > 0:
        return jnp.concatenate([edge, values[..., :-1]], axis=-1)
    return jnp.concatenate([values[..., 1:], edge], axis=-1)


def transport(center, neighbours, speeds, positive, fluid):
    middle = center.astype(jnp.float32)
    flux = jnp.zeros_like(middle)
    for component, (low, high) in enumerate(neighbours):
        upstream = jnp.where(positive[component][:, None, None], low, high).astype(jnp.float32)
        flux = flux + speeds[component][:, None, None] * (middle - upstream)
    return (middle - fluid[None] * flux).astype(jnp.bfloat16)


def on_device(distribution, collision, speeds, directions, cell_flags):
    velocities = collision.shape[0]
    chunk = velocities // CHUNKS
    planes = lax.all_gather(distribution, "vout", axis=0, tiled=True)
    planes = planes.reshape((planes.shape[0] // CORES, CORES) + planes.shape[1:])
    core = lax.rem(lax.axis_index("vin"), CORES)
    mine = lax.dynamic_index_in_dim(planes, core, 1, keepdims=False)
    theirs = lax.dynamic_index_in_dim(planes, 1 - core, 1, keepdims=False)
    fluid = (1 - cell_flags[0]).astype(jnp.float32)
    outs = []
    for part in range(CHUNKS):
        own = slice(part * chunk, (part + 1) * chunk)
        block = collision[own]
        spec = "vu,zuyx->zvyx"
        away = jnp.einsum(spec, block, theirs, preferred_element_type=jnp.float32)
        near = jnp.einsum(spec, block, mine, preferred_element_type=jnp.float32)
        got = hop(away.astype(jnp.bfloat16), "vin", core_pairs("vin"))
        both = (near + got.astype(jnp.float32)).astype(jnp.bfloat16)
        cells = scatter_line(both, "vin")
        before = from_lower(cells[:, -1:], "cell")
        after = from_higher(cells[:, :1], "cell")
        neighbours = (
            (shifted(cells, 1), shifted(cells, -1)),
            (
                jnp.concatenate([before, cells[:, :-1]], axis=1),
                jnp.concatenate([cells[:, 1:], after], axis=1),
            ),
            (from_lower(cells, "vin"), from_higher(cells, "vin")),
        )
        outs.append(transport(cells, neighbours, speeds[:, own], directions[:, own] == 1, fluid))
    return jnp.concatenate(outs, axis=0)[None]


def solution(mesh):
    return jax.shard_map(
        on_device,
        mesh=mesh,
        in_specs=(
            P("vout", "vin", "cell", None),
            P("vout", "vin"),
            P(None, "vout"),
            P(None, "vout"),
            P("vin", "cell", None),
        ),
        out_specs=P("vin", "vout", "cell", None),
        check_vma=False,
    )
```

profile of v0, /device:TPU:8, one launch (start us, length us, event | category | flops | bytes accessed | tf_op | source)
XLA Modules:
  0.0 504.9 jit_solution(819726647843778147)
XLA Ops:
  10.8 90.5 %all-gather.2.cloned.1.call-done = bf16[8,1728,2,128]{3,1,2,0:T(8,128)(2,1)} async-done(((bf16[4,1728,2,128]{3,1,2,0:T(8,128)(2,1)}), bf16[8,1728,2,128]{3,1,2,0:T(8,128)(2,1)}) %all-gather.2.cloned.1.call-update) | async-done | bytes 7077904 | tf_op jit(solution)/shard_map/all_gather | solution.py:73
  101.4 14.5 %fusion.42 = bf16[4,2304,2,128]{1,3,2,0:T(8,128)(2,1)} fusion(bf16[6912,1728]{0,1:T(8,128)(2,1)} %param.6, bf16[4,2,1728,2,128]{4,2,3,1,0:T(8,128)(2,1)} %bitcast.137, s32[]{:T(128)S(6)} %select_n.67), kind=kOutput, calls=%fused_computation.29 | convolution fusion | flops 8156086272 | bytes 16220164 | tf_op jit(solution)/shard_map/vu,zuyx->zvyx/dot_general | solution.py:84
  115.9 13.7 %fusion.39 = bf16[4,2304,2,128]{1,3,2,0:T(8,128)(2,1)} fusion(bf16[6912,1728]{0,1:T(8,128)(2,1)} %param.6, bf16[4,2,1728,2,128]{4,2,3,1,0:T(8,128)(2,1)S(1)} %bitcast.141, s32[]{:T(128)S(6)} %select_n.67), kind=kOutput, calls=%fused_computation.28 | convolution fusion | flops 8156086272 | bytes 16220164 | tf_op jit(solution)/shard_map/vu,zuyx->zvyx/dot_general | solution.py:84
  130.1 14.2 %fusion.36 = bf16[4,2304,2,128]{1,3,2,0:T(8,128)(2,1)} fusion(bf16[6912,1728]{0,1:T(8,128)(2,1)} %param.6, bf16[4,2,1728,2,128]{4,2,3,1,0:T(8,128)(2,1)S(1)} %bitcast.142, s32[]{:T(128)S(6)} %select_n.67), kind=kOutput, calls=%fused_computation.27 | convolution fusion | flops 8156086272 | bytes 16220164 | tf_op jit(solution)/shard_map/vu,zuyx->zvyx/dot_general | solution.py:84
  145.0 13.6 %fusion.2 = bf16[4,2304,2,128]{1,3,2,0:T(8,128)(2,1)S(1)} fusion(bf16[4,2304,2,128]{1,3,2,0:T(8,128)(2,1)} %collective-permute-done, bf16[6912,1728]{0,1:T(8,128)(2,1)} %param.6, bf16[4,2,1728,2,128]{4,2,3,1,0:T(8,128)(2,1)} %bitcast.138, s32[]{:T(128)S(6)} %select_n.66), kind=kOutput, calls=%fused_computation.5 | convolution fusion | flops 8160804864 | bytes 20938756 | tf_op jit(solution)/shard_map/vu,zuyx->zvyx/dot_general | solution.py:85
  161.7 13.7 %fusion.1 = bf16[4,2304,2,128]{1,3,2,0:T(8,128)(2,1)S(1)} fusion(bf16[4,2304,2,128]{1,3,2,0:T(8,128)(2,1)} %collective-permute-done.11, bf16[6912,1728]{0,1:T(8,128)(2,1)} %param.6, bf16[4,2,1728,2,128]{4,2,3,1,0:T(8,128)(2,1)} %bitcast.139, s32[]{:T(128)S(6)} %select_n.66), kind=kOutput, calls=%fused_computation.3 | convolution fusion | flops 8160804864 | bytes 20938756 | tf_op jit(solution)/shard_map/vu,zuyx->zvyx/dot_general | solution.py:85
  178.6 13.6 %fusion = bf16[4,2304,2,128]{1,3,2,0:T(8,128)(2,1)S(1)} fusion(bf16[4,2304,2,128]{1,3,2,0:T(8,128)(2,1)} %collective-permute-done.22, bf16[6912,1728]{0,1:T(8,128)(2,1)} %param.6, bf16[4,2,1728,2,128]{4,2,3,1,0:T(8,128)(2,1)} %bitcast.140, s32[]{:T(128)S(6)} %select_n.66), kind=kOutput, calls=%fused_computation.1 | convolution fusion | flops 8160804864 | bytes 20938756 | tf_op jit(solution)/shard_map/vu,zuyx->zvyx/dot_general | solution.py:85
  194.7 20.1 %collective-permute-done.12 = bf16[2304,2,128]{0,2,1:T(8,128)(2,1)} collective-permute-done((bf16[2304,2,128]{0,2,1:T(8,128)(2,1)S(1)}, bf16[2304,2,128]{0,2,1:T(8,128)(2,1)}, u32[]{:S(2)}, u32[]{:S(2)}) %collective-permute-start.12) | collective-permute-done | bytes 1179680 | tf_op jit(solution)/shard_map/ppermute | solution.py:21
  218.3 21.7 %collective-permute-done.23 = bf16[2304,2,128]{0,2,1:T(8,128)(2,1)S(1)} collective-permute-done((bf16[2304,2,128]{0,2,1:T(8,128)(2,1)S(1)}, bf16[2304,2,128]{0,2,1:T(8,128)(2,1)S(1)}, u32[]{:S(2)}, u32[]{:S(2)}) %collective-permute-start.23) | collective-permute-done | bytes 1179680 | tf_op jit(solution)/shard_map/ppermute | solution.py:21
  244.1 21.1 %collective-permute-done.2 = bf16[2304,2,128]{0,2,1:T(8,128)(2,1)S(1)} collective-permute-done((bf16[2304,2,128]{0,2,1:T(8,128)(2,1)S(1)}, bf16[2304,2,128]{0,2,1:T(8,128)(2,1)S(1)}, u32[]{:S(2)}, u32[]{:S(2)}) %collective-permute-start.2) | collective-permute-done | bytes 1179680 | tf_op jit(solution)/shard_map/ppermute | solution.py:21
  268.4 4.8 collective-permute-start.3
  273.2 17.3 %collective-permute-done.13 = bf16[2304,2,128]{0,2,1:T(8,128)(2,1)S(1)} collective-permute-done((bf16[2304,2,128]{0,2,1:T(8,128)(2,1)S(1)}, bf16[2304,2,128]{0,2,1:T(8,128)(2,1)S(1)}, u32[]{:S(2)}, u32[]{:S(2)}) %collective-permute-start.13) | collective-permute-done | bytes 1179680 | tf_op jit(solution)/shard_map/ppermute | solution.py:21
  293.7 4.6 collective-permute-start.14
  298.2 17.5 %collective-permute-done.24 = bf16[2304,2,128]{0,2,1:T(8,128)(2,1)S(1)} collective-permute-done((bf16[2304,2,128]{0,2,1:T(8,128)(2,1)S(1)}, bf16[2304,2,128]{0,2,1:T(8,128)(2,1)S(1)}, u32[]{:S(2)}, u32[]{:S(2)}) %collective-permute-start.24) | collective-permute-done | bytes 1179680 | tf_op jit(solution)/shard_map/ppermute | solution.py:21
  317.7 4.6 collective-permute-start.25
  324.9 23.0 %collective-permute-done.27 = bf16[2304,2,128]{0,2,1:T(8,128)(2,1)S(1)} collective-permute-done((bf16[2304,2,128]{0,2,1:T(8,128)(2,1)S(1)}, bf16[2304,2,128]{0,2,1:T(8,128)(2,1)S(1)}, u32[]{:S(2)}, u32[]{:S(2)}) %collective-permute-start.27) | collective-permute-done | bytes 1179680 | tf_op jit(solution)/shard_map/ppermute | solution.py:21
  352.0 21.1 %collective-permute-done.6 = bf16[2304,2,128]{0,2,1:T(8,128)(2,1)S(1)} collective-permute-done((bf16[2304,2,128]{0,2,1:T(8,128)(2,1)S(1)}, bf16[2304,2,128]{0,2,1:T(8,128)(2,1)S(1)}, u32[]{:S(2)}, u32[]{:S(2)}) %collective-permute-start.6) | collective-permute-done | bytes 1179680 | tf_op jit(solution)/shard_map/ppermute | solution.py:21
  378.3 20.2 %collective-permute-done.17 = bf16[2304,2,128]{0,2,1:T(8,128)(2,1)S(1)} collective-permute-done((bf16[2304,2,128]{0,2,1:T(8,128)(2,1)S(1)}, bf16[2304,2,128]{0,2,1:T(8,128)(2,1)S(1)}, u32[]{:S(2)}, u32[]{:S(2)}) %collective-permute-start.17) | collective-permute-done | bytes 1179680 | tf_op jit(solution)/shard_map/ppermute | solution.py:21
  404.7 17.9 %collective-permute-done.28 = bf16[2304,2,128]{0,2,1:T(8,128)(2,1)S(1)} collective-permute-done((bf16[2304,2,128]{0,2,1:T(8,128)(2,1)S(1)}, bf16[2304,2,128]{0,2,1:T(8,128)(2,1)S(1)}, u32[]{:S(2)}, u32[]{:S(2)}) %collective-permute-start.28) | collective-permute-done | bytes 1179680 | tf_op jit(solution)/shard_map/ppermute | solution.py:21
  426.5 12.0 %collective-permute-done.8 = bf16[2304,1,128]{0,2,1:T(8,128)(2,1)S(1)} collective-permute-done((bf16[2304,1,128]{0,2,1:T(8,128)(2,1)S(1)}, bf16[2304,1,128]{0,2,1:T(8,128)(2,1)S(1)}, u32[]{:S(2)}, u32[]{:S(2)}) %collective-permute-start.8) | collective-permute-done | bytes 589856 | tf_op jit(solution)/shard_map/ppermute | solution.py:17
  440.1 10.7 %collective-permute-done.18 = bf16[2304,1,128]{0,2,1:T(8,128)(2,1)S(1)} collective-permute-done((bf16[2304,1,128]{0,2,1:T(8,128)(2,1)S(1)}, bf16[2304,1,128]{0,2,1:T(8,128)(2,1)S(1)}, u32[]{:S(2)}, u32[]{:S(2)}) %collective-permute-start.18) | collective-permute-done | bytes 589856 | tf_op jit(solution)/shard_map/ppermute | solution.py:12
  459.9 12.5 %collective-permute-done.19 = bf16[2304,1,128]{0,2,1:T(8,128)(2,1)S(1)} collective-permute-done((bf16[2304,1,128]{0,2,1:T(8,128)(2,1)S(1)}, bf16[2304,1,128]{0,2,1:T(8,128)(2,1)S(1)}, u32[]{:S(2)}, u32[]{:S(2)}) %collective-permute-start.19) | collective-permute-done | bytes 589856 | tf_op jit(solution)/shard_map/ppermute | solution.py:17
  477.4 7.3 %collective-permute-done.29 = bf16[2304,1,128]{0,2,1:T(8,128)(2,1)S(1)} collective-permute-done((bf16[2304,1,128]{0,2,1:T(8,128)(2,1)S(1)}, bf16[2304,1,128]{0,2,1:T(8,128)(2,1)S(1)}, u32[]{:S(2)}, u32[]{:S(2)}) %collective-permute-start.29) | collective-permute-done | bytes 589856 | tf_op jit(solution)/shard_map/ppermute | solution.py:12
  491.3 6.5 %copy.12 = bf16[1,6912,2,128]{3,2,1,0:T(2,128)(2,1)} copy(bf16[1,6912,2,128]{1,3,2,0:T(8,128)(2,1)S(1)} %maximum_bitcast_fusion) | data formatting | bytes 7077888 | tf_op jit(solution)/shard_map/broadcast_in_dim | solution.py:100
  (92 shorter events, 74.1 us)
Async XLA Ops:
  6.5 94.8 %all-gather.2.cloned.1.call-start = ((), (), s32[]{:S(2)}) async-start(), calls=%async_computation | async-start | bytes 10616832 | tf_op jit(solution)/shard_map/all_gather | solution.py:73
  144.3 34.3 %collective-permute-start.22 = (bf16[4,2304,2,128]{1,3,2,0:T(8,128)(2,1)}, bf16[4,2304,2,128]{1,3,2,0:T(8,128)(2,1)}, u32[]{:S(2)}, u32[]{:S(2)}) collective-permute-start(bf16[4,2304,2,128]{1,3,2,0:T(8,128)(2,1)} %fusion.36), channel_id=1, source_target_pairs={{0,4},{4,0},{8,12},{12,8},{16,20},{20,16},{24,28},{28,24},{1,5},{5... | collective-permute-start | bytes 14155784 | tf_op jit(solution)/shard_map/ppermute | solution.py:21
  158.7 34.9 %collective-permute-start.1 = (bf16[2304,2,128]{0,2,1:T(8,128)(2,1)S(1)}, bf16[2304,2,128]{0,2,1:T(8,128)(2,1)S(1)}, u32[]{:S(2)}, u32[]{:S(2)}) collective-permute-start(bf16[2304,2,128]{0,2,1:T(8,128)(2,1)S(1)} %get-tuple-element.25), channel_id=1, source_target_pairs={{0,8},{4,12},{1,9},{5,13},{2,10},{6,14},{3,11},{7,15}} | collective-permute-start | bytes 3538952 | tf_op jit(solution)/shard_map/ppermute | solution.py:21
  160.0 82.2 %collective-permute-start.4 = (bf16[2304,2,128]{0,2,1:T(8,128)(2,1)S(1)}, bf16[2304,2,128]{0,2,1:T(8,128)(2,1)}, u32[]{:S(2)}, u32[]{:S(2)}) collective-permute-start(bf16[2304,2,128]{0,2,1:T(8,128)(2,1)S(1)} %get-tuple-element.26), channel_id=1, source_target_pairs={{24,16},{28,20},{25,17},{29,21},{26,18},{30,22},{27,19},{31,23}} | collective-permute-start | bytes 3538952 | tf_op jit(solution)/shard_map/ppermute | solution.py:21
  175.6 39.2 %collective-permute-start.12 = (bf16[2304,2,128]{0,2,1:T(8,128)(2,1)S(1)}, bf16[2304,2,128]{0,2,1:T(8,128)(2,1)}, u32[]{:S(2)}, u32[]{:S(2)}) collective-permute-start(bf16[2304,2,128]{0,2,1:T(8,128)(2,1)S(1)} %get-tuple-element.29), channel_id=1, source_target_pairs={{0,8},{4,12},{1,9},{5,13},{2,10},{6,14},{3,11},{7,15}} | collective-permute-start | bytes 3538952 | tf_op jit(solution)/shard_map/ppermute | solution.py:21
  176.9 91.5 %collective-permute-start.15 = (bf16[2304,2,128]{0,2,1:T(8,128)(2,1)S(1)}, bf16[2304,2,128]{0,2,1:T(8,128)(2,1)}, u32[]{:S(2)}, u32[]{:S(2)}) collective-permute-start(bf16[2304,2,128]{0,2,1:T(8,128)(2,1)S(1)} %get-tuple-element.30), channel_id=1, source_target_pairs={{24,16},{28,20},{25,17},{29,21},{26,18},{30,22},{27,19},{31,23}} | collective-permute-start | bytes 3538952 | tf_op jit(solution)/shard_map/ppermute | solution.py:21
  192.3 47.6 %collective-permute-start.23 = (bf16[2304,2,128]{0,2,1:T(8,128)(2,1)S(1)}, bf16[2304,2,128]{0,2,1:T(8,128)(2,1)S(1)}, u32[]{:S(2)}, u32[]{:S(2)}) collective-permute-start(bf16[2304,2,128]{0,2,1:T(8,128)(2,1)S(1)} %get-tuple-element.33), channel_id=1, source_target_pairs={{0,8},{4,12},{1,9},{5,13},{2,10},{6,14},{3,11},{7,15}} | collective-permute-start | bytes 3538952 | tf_op jit(solution)/shard_map/ppermute | solution.py:21
  193.6 100.0 %collective-permute-start.26 = (bf16[2304,2,128]{0,2,1:T(8,128)(2,1)S(1)}, bf16[2304,2,128]{0,2,1:T(8,128)(2,1)S(1)}, u32[]{:S(2)}, u32[]{:S(2)}) collective-permute-start(bf16[2304,2,128]{0,2,1:T(8,128)(2,1)S(1)} %get-tuple-element.34), channel_id=1, source_target_pairs={{24,16},{28,20},{25,17},{29,21},{26,18},{30,22},{27,19},{31,23}} | collective-permute-start | bytes 3538952 | tf_op jit(solution)/shard_map/ppermute | solution.py:21
  214.8 50.5 %collective-permute-start.2 = (bf16[2304,2,128]{0,2,1:T(8,128)(2,1)S(1)}, bf16[2304,2,128]{0,2,1:T(8,128)(2,1)S(1)}, u32[]{:S(2)}, u32[]{:S(2)}) collective-permute-start(bf16[2304,2,128]{0,2,1:T(8,128)(2,1)S(1)} %fusion.92), channel_id=1, source_target_pairs={{0,8},{4,12},{8,16},{12,20},{1,9},{5,13},{9,17},{13,21},{2,10},{6,... | collective-permute-start | bytes 3538952 | tf_op jit(solution)/shard_map/ppermute | solution.py:21
  239.9 50.6 %collective-permute-start.13 = (bf16[2304,2,128]{0,2,1:T(8,128)(2,1)S(1)}, bf16[2304,2,128]{0,2,1:T(8,128)(2,1)S(1)}, u32[]{:S(2)}, u32[]{:S(2)}) collective-permute-start(bf16[2304,2,128]{0,2,1:T(8,128)(2,1)S(1)} %fusion.86), channel_id=1, source_target_pairs={{0,8},{4,12},{8,16},{12,20},{1,9},{5,13},{9,17},{13,21},{2,10},{6,... | collective-permute-start | bytes 3538952 | tf_op jit(solution)/shard_map/ppermute | solution.py:21
  242.2 73.6 %collective-permute-start.24 = (bf16[2304,2,128]{0,2,1:T(8,128)(2,1)S(1)}, bf16[2304,2,128]{0,2,1:T(8,128)(2,1)S(1)}, u32[]{:S(2)}, u32[]{:S(2)}) collective-permute-start(bf16[2304,2,128]{0,2,1:T(8,128)(2,1)S(1)} %fusion.80), channel_id=1, source_target_pairs={{0,8},{4,12},{8,16},{12,20},{1,9},{5,13},{9,17},{13,21},{2,10},{6,... | collective-permute-start | bytes 3538952 | tf_op jit(solution)/shard_map/ppermute | solution.py:21
  267.1 50.6 %collective-permute-start.5 = (bf16[2304,2,128]{0,2,1:T(8,128)(2,1)S(1)}, bf16[2304,2,128]{0,2,1:T(8,128)(2,1)S(1)}, u32[]{:S(2)}, u32[]{:S(2)}) collective-permute-start(bf16[2304,2,128]{0,2,1:T(8,128)(2,1)S(1)} %get-tuple-element.24), channel_id=1, source_target_pairs={{24,16},{28,20},{16,8},{20,12},{25,17},{29,21},{17,9},{21,13},{26,... | collective-permute-start | bytes 3538952 | tf_op jit(solution)/shard_map/ppermute | solution.py:21
  268.4 81.7 %collective-permute-start.3 = (bf16[2304,2,128]{0,2,1:T(8,128)(2,1)S(1)}, bf16[2304,2,128]{0,2,1:T(8,128)(2,1)S(1)}, u32[]{:S(2)}, u32[]{:S(2)}) collective-permute-start(bf16[2304,2,128]{0,2,1:T(8,128)(2,1)S(1)} %get-tuple-element.23), channel_id=1, source_target_pairs={{0,8},{4,12},{8,16},{12,20},{16,24},{20,28},{1,9},{5,13},{9,17},{1... | collective-permute-start | bytes 3538952 | tf_op jit(solution)/shard_map/ppermute | solution.py:21
  293.7 82.2 %collective-permute-start.14 = (bf16[2304,2,128]{0,2,1:T(8,128)(2,1)S(1)}, bf16[2304,2,128]{0,2,1:T(8,128)(2,1)S(1)}, u32[]{:S(2)}, u32[]{:S(2)}) collective-permute-start(bf16[2304,2,128]{0,2,1:T(8,128)(2,1)S(1)} %get-tuple-element.27), channel_id=1, source_target_pairs={{0,8},{4,12},{8,16},{12,20},{16,24},{20,28},{1,9},{5,13},{9,17},{1... | collective-permute-start | bytes 3538952 | tf_op jit(solution)/shard_map/ppermute | solution.py:21
  317.7 83.6 %collective-permute-start.25 = (bf16[2304,2,128]{0,2,1:T(8,128)(2,1)S(1)}, bf16[2304,2,128]{0,2,1:T(8,128)(2,1)S(1)}, u32[]{:S(2)}, u32[]{:S(2)}) collective-permute-start(bf16[2304,2,128]{0,2,1:T(8,128)(2,1)S(1)} %get-tuple-element.31), channel_id=1, source_target_pairs={{0,8},{4,12},{8,16},{12,20},{16,24},{20,28},{1,9},{5,13},{9,17},{1... | collective-permute-start | bytes 3538952 | tf_op jit(solution)/shard_map/ppermute | solution.py:21
  322.6 50.6 %collective-permute-start.6 = (bf16[2304,2,128]{0,2,1:T(8,128)(2,1)S(1)}, bf16[2304,2,128]{0,2,1:T(8,128)(2,1)S(1)}, u32[]{:S(2)}, u32[]{:S(2)}) collective-permute-start(bf16[2304,2,128]{0,2,1:T(8,128)(2,1)S(1)} %fusion.91), channel_id=1, source_target_pairs={{24,16},{28,20},{16,8},{20,12},{8,0},{12,4},{25,17},{29,21},{17,9}... | collective-permute-start | bytes 3538952 | tf_op jit(solution)/shard_map/ppermute | solution.py:21
  347.9 50.6 %collective-permute-start.17 = (bf16[2304,2,128]{0,2,1:T(8,128)(2,1)S(1)}, bf16[2304,2,128]{0,2,1:T(8,128)(2,1)S(1)}, u32[]{:S(2)}, u32[]{:S(2)}) collective-permute-start(bf16[2304,2,128]{0,2,1:T(8,128)(2,1)S(1)} %fusion.85), channel_id=1, source_target_pairs={{24,16},{28,20},{16,8},{20,12},{8,0},{12,4},{25,17},{29,21},{17,9}... | collective-permute-start | bytes 3538952 | tf_op jit(solution)/shard_map/ppermute | solution.py:21
  350.1 72.4 %collective-permute-start.28 = (bf16[2304,2,128]{0,2,1:T(8,128)(2,1)S(1)}, bf16[2304,2,128]{0,2,1:T(8,128)(2,1)S(1)}, u32[]{:S(2)}, u32[]{:S(2)}) collective-permute-start(bf16[2304,2,128]{0,2,1:T(8,128)(2,1)S(1)} %fusion.79), channel_id=1, source_target_pairs={{24,16},{28,20},{16,8},{20,12},{8,0},{12,4},{25,17},{29,21},{17,9}... | collective-permute-start | bytes 3538952 | tf_op jit(solution)/shard_map/ppermute | solution.py:21
  373.6 79.0 %collective-permute-start.10 = (bf16[2304,2,128]{0,2,1:T(8,128)(2,1)S(1)}, bf16[2304,2,128]{0,2,1:T(8,128)(2,1)S(1)}, u32[]{:S(2)}, u32[]{:S(2)}) collective-permute-start(bf16[2304,2,128]{0,2,1:T(8,128)(2,1)S(1)} %fusion.95), channel_id=1, source_target_pairs={{4,0},{8,4},{12,8},{16,12},{20,16},{24,20},{28,24},{5,1},{9,5},{13... | collective-permute-start | bytes 3538952 | tf_op jit(solution)/shard_map/ppermute | solution.py:17
  375.9 80.5 %collective-permute-start.9 = (bf16[2304,2,128]{0,2,1:T(8,128)(2,1)S(1)}, bf16[2304,2,128]{0,2,1:T(8,128)(2,1)S(1)}, u32[]{:S(2)}, u32[]{:S(2)}) collective-permute-start(bf16[2304,2,128]{0,2,1:T(8,128)(2,1)S(1)} %fusion.95), channel_id=1, source_target_pairs={{0,4},{4,8},{8,12},{12,16},{16,20},{20,24},{24,28},{1,5},{5,9},{9,... | collective-permute-start | bytes 3538952 | tf_op jit(solution)/shard_map/ppermute | solution.py:12
  398.9 74.9 %collective-permute-start.20 = (bf16[2304,2,128]{0,2,1:T(8,128)(2,1)S(1)}, bf16[2304,2,128]{0,2,1:T(8,128)(2,1)S(1)}, u32[]{:S(2)}, u32[]{:S(2)}) collective-permute-start(bf16[2304,2,128]{0,2,1:T(8,128)(2,1)S(1)} %fusion.89), channel_id=1, source_target_pairs={{0,4},{4,8},{8,12},{12,16},{16,20},{20,24},{24,28},{1,5},{5,9},{9,... | collective-permute-start | bytes 3538952 | tf_op jit(solution)/shard_map/ppermute | solution.py:12
  424.6 50.6 %collective-permute-start.21 = (bf16[2304,2,128]{0,2,1:T(8,128)(2,1)S(1)}, bf16[2304,2,128]{0,2,1:T(8,128)(2,1)S(1)}, u32[]{:S(2)}, u32[]{:S(2)}) collective-permute-start(bf16[2304,2,128]{0,2,1:T(8,128)(2,1)S(1)} %fusion.89), channel_id=1, source_target_pairs={{4,0},{8,4},{12,8},{16,12},{20,16},{24,20},{28,24},{5,1},{9,5},{13... | collective-permute-start | bytes 3538952 | tf_op jit(solution)/shard_map/ppermute | solution.py:17
  450.8 38.1 %collective-permute-start.31 = (bf16[2304,2,128]{0,2,1:T(8,128)(2,1)S(1)}, bf16[2304,2,128]{0,2,1:T(8,128)(2,1)S(1)}, u32[]{:S(2)}, u32[]{:S(2)}) collective-permute-start(bf16[2304,2,128]{0,2,1:T(8,128)(2,1)S(1)} %fusion.83), channel_id=1, source_target_pairs={{0,4},{4,8},{8,12},{12,16},{16,20},{20,24},{24,28},{1,5},{5,9},{9,... | collective-permute-start | bytes 3538952 | tf_op jit(solution)/shard_map/ppermute | solution.py:12
  452.7 36.1 %collective-permute-start.32 = (bf16[2304,2,128]{0,2,1:T(8,128)(2,1)S(1)}, bf16[2304,2,128]{0,2,1:T(8,128)(2,1)S(1)}, u32[]{:S(2)}, u32[]{:S(2)}) collective-permute-start(bf16[2304,2,128]{0,2,1:T(8,128)(2,1)S(1)} %fusion.83), channel_id=1, source_target_pairs={{4,0},{8,4},{12,8},{16,12},{20,16},{24,20},{28,24},{5,1},{9,5},{13... | collective-permute-start | bytes 3538952 | tf_op jit(solution)/shard_map/ppermute | solution.py:17
  (14 other events, 277.5 us)
Sparse Core Ops, SparseCore 0:
  10.9 90.3 all-gather.1
where the time goes:
time: 513 us; the launch traced here: 505 us
  waiting for transfers between devices  317 us (62%)
  matrix products  83.3 us (16%)
  starting transfers between devices  61.7 us (12%)
  other arithmetic  15.7 us (3%)
  between operations  14.2 us (3%)
  local copies, waits for them, and re-layouts  12.8 us (2%)
    ppermute x21, waiting for transfers between devices, hop(): return lax.ppermute(values, axis, pairs)  180 us
    all_gather x1, waiting for transfers between devices, on_device(): planes = lax.all_gather(distribution, 'vout', axis=0, tiled=True)  90.5 us
    dot_general x3, matrix products, on_device(): away = jnp.einsum(spec, block, theirs, preferred_element_type=jnp.float32)  42.4 us
    dot_general x3, matrix products, on_device(): near = jnp.einsum(spec, block, mine, preferred_element_type=jnp.float32)  40.9 us
    ppermute x21, starting transfers between devices, hop(): return lax.ppermute(values, axis, pairs)  37.7 us
    ppermute x6, waiting for transfers between devices, from_higher(): return lax.ppermute(values, axis, [(i + 1, i) for i in range(ends)])  28.7 us
    ppermute x6, waiting for transfers between devices, from_lower(): return lax.ppermute(values, axis, [(i, i + 1) for i in range(ends)])  18 us
    ppermute x6, starting transfers between devices, from_lower(): return lax.ppermute(values, axis, [(i, i + 1) for i in range(ends)])  12.6 us
  transfers between devices with their start and end apart: 34, of which 16 were waited for; matrix products, arithmetic and copies ran while one was open for 17% of the time, Pallas kernels for 0%

commit v1 on v0

--- a/solution.py
+++ b/solution.py
@@ -70,7 +70,15 @@
 def on_device(distribution, collision, speeds, directions, cell_flags):
     velocities = collision.shape[0]
     chunk = velocities // CHUNKS
-    planes = lax.all_gather(distribution, "vout", axis=0, tiled=True)
+    ways, here, k = (lax.axis_size("vout"), lax.axis_index("vout"), distribution.shape[0])
+    line, have = (distribution, 1)
+    while have < ways:
+        line = jnp.concatenate(
+            [line, lax.ppermute(line, "vout", [(d, (d - have) % ways) for d in range(ways)])],
+            axis=0,
+        )
+        have = 2 * have
+    planes = jnp.roll(line, here * k, axis=0)
     planes = planes.reshape((planes.shape[0] // CORES, CORES) + planes.shape[1:])
     core = lax.rem(lax.axis_index("vin"), CORES)
     mine = lax.dynamic_index_in_dim(planes, core, 1, keepdims=False)

time: 513 us -> 494 us (0.963)
  waiting for transfers between devices: 317 us -> 302 us
  between operations: 14.2 us -> 0.84 us
  other arithmetic: 15.7 us -> 21.7 us
    all_gather x1 -> x0, waiting for transfers between devices: 90.5 us -> none  [on_device(): planes = lax.all_gather(distribution, 'vout', axis=0, tiled=True)]
    ppermute x0 -> x1, waiting for transfers between devices: none -> 76.9 us  [on_device(): lax.ppermute(line, 'vout', [(d, (d - have) % ways) for d in range(ways)])]
    concatenate x0 -> x1, other arithmetic: none -> 6.04 us  [on_device(): planes = jnp.roll(line, here * k, axis=0)]
where the time goes in v1:
time: 494 us; the launch traced here: 485 us
  waiting for transfers between devices  302 us (61%)
  matrix products  85 us (17%)
  starting transfers between devices  64.5 us (13%)
  other arithmetic  21.7 us (4%)
  local copies, waits for them, and re-layouts  11 us (2%)
    ppermute x21, waiting for transfers between devices, hop(): return lax.ppermute(values, axis, pairs)  179 us
    ppermute x1, waiting for transfers between devices, on_device(): lax.ppermute(line, 'vout', [(d, (d - have) % ways) for d in range(ways)])  76.9 us
    dot_general x3, matrix products, on_device(): away = jnp.einsum(spec, block, theirs, preferred_element_type=jnp.float32)  44.2 us
    dot_general x3, matrix products, on_device(): near = jnp.einsum(spec, block, mine, preferred_element_type=jnp.float32)  40.9 us
    ppermute x21, starting transfers between devices, hop(): return lax.ppermute(values, axis, pairs)  37.7 us
    ppermute x6, waiting for transfers between devices, from_higher(): return lax.ppermute(values, axis, [(i + 1, i) for i in range(ends)])  28.6 us
    ppermute x6, waiting for transfers between devices, from_lower(): return lax.ppermute(values, axis, [(i, i + 1) for i in range(ends)])  18 us
    ppermute x6, starting transfers between devices, from_higher(): return lax.ppermute(values, axis, [(i + 1, i) for i in range(ends)])  13.1 us
  transfers between devices with their start and end apart: 34, of which 16 were waited for; matrix products, arithmetic and copies ran while one was open for 17% of the time, Pallas kernels for 0%

profile of v1, /device:TPU:8, one launch (start us, length us, event | category | flops | bytes accessed | tf_op | source)
XLA Modules:
  0.0 485.4 jit_solution(18411083895661937374)
XLA Ops:
  4.0 76.9 %collective-permute-done = bf16[4,1728,2,128]{3,1,2,0:T(8,128)(2,1)} collective-permute-done((bf16[4,1728,2,128]{3,1,2,0:T(8,128)(2,1)S(1)}, bf16[4,1728,2,128]{3,1,2,0:T(8,128)(2,1)}, u32[]{:S(2)}, u32[]{:S(2)}) %collective-permute-start) | collective-permute-done | bytes 3538976 | tf_op jit(solution)/shard_map/ppermute | solution.py:77
  80.9 6.0 %fusion.17 = bf16[8,1728,2,128]{3,1,2,0:T(8,128)(2,1)S(1)} fusion(s32[]{:T(128)S(6)} %select_n.79, bf16[4,1728,2,128]{3,1,2,0:T(8,128)(2,1)S(1)} %copy.8, bf16[4,1728,2,128]{3,1,2,0:T(8,128)(2,1)} %collective-permute-done), kind=kLoop, calls=%fused_computation.24 | loop fusion | flops 10616832 | bytes 14155780 | tf_op jit(solution)/shard_map/jit(_roll_dynamic)/concatenate | solution.py:81
  87.0 16.4 %fusion.45 = bf16[4,2304,2,128]{1,3,2,0:T(8,128)(2,1)} fusion(bf16[6912,1728]{0,1:T(8,128)(2,1)} %param.6, bf16[4,2,1728,2,128]{4,2,3,1,0:T(8,128)(2,1)S(1)} %bitcast.133, s32[]{:T(128)S(6)} %select_n.81), kind=kOutput, calls=%fused_computation.36 | convolution fusion | flops 8156086272 | bytes 16220164 | tf_op jit(solution)/shard_map/vu,zuyx->zvyx/dot_general | solution.py:92
  103.3 13.7 %fusion.42 = bf16[4,2304,2,128]{1,3,2,0:T(8,128)(2,1)} fusion(bf16[6912,1728]{0,1:T(8,128)(2,1)} %param.6, bf16[4,2,1728,2,128]{4,2,3,1,0:T(8,128)(2,1)S(1)} %bitcast.134, s32[]{:T(128)S(6)} %select_n.81), kind=kOutput, calls=%fused_computation.35 | convolution fusion | flops 8156086272 | bytes 16220164 | tf_op jit(solution)/shard_map/vu,zuyx->zvyx/dot_general | solution.py:92
  117.5 14.1 %fusion.39 = bf16[4,2304,2,128]{1,3,2,0:T(8,128)(2,1)} fusion(bf16[6912,1728]{0,1:T(8,128)(2,1)} %param.6, bf16[4,2,1728,2,128]{4,2,3,1,0:T(8,128)(2,1)S(1)} %bitcast.135, s32[]{:T(128)S(6)} %select_n.81), kind=kOutput, calls=%fused_computation.34 | convolution fusion | flops 8156086272 | bytes 16220164 | tf_op jit(solution)/shard_map/vu,zuyx->zvyx/dot_general | solution.py:92
  132.3 13.6 %fusion.2 = bf16[4,2304,2,128]{1,3,2,0:T(8,128)(2,1)S(1)} fusion(bf16[4,2304,2,128]{1,3,2,0:T(8,128)(2,1)} %collective-permute-done.1, bf16[6912,1728]{0,1:T(8,128)(2,1)} %param.6, bf16[4,2,1728,2,128]{4,2,3,1,0:T(8,128)(2,1)} %bitcast.136, s32[]{:T(128)S(6)} %select_n.80), kind=kOutput, calls=%fused_computation.9 | convolution fusion | flops 8160804864 | bytes 20938756 | tf_op jit(solution)/shard_map/vu,zuyx->zvyx/dot_general | solution.py:93
  149.0 13.7 %fusion.1 = bf16[4,2304,2,128]{1,3,2,0:T(8,128)(2,1)S(1)} fusion(bf16[4,2304,2,128]{1,3,2,0:T(8,128)(2,1)} %collective-permute-done.12, bf16[6912,1728]{0,1:T(8,128)(2,1)} %param.6, bf16[4,2,1728,2,128]{4,2,3,1,0:T(8,128)(2,1)} %bitcast.137, s32[]{:T(128)S(6)} %select_n.80), kind=kOutput, calls=%fused_computation.7 | convolution fusion | flops 8160804864 | bytes 20938756 | tf_op jit(solution)/shard_map/vu,zuyx->zvyx/dot_general | solution.py:93
  165.9 13.6 %fusion = bf16[4,2304,2,128]{1,3,2,0:T(8,128)(2,1)S(1)} fusion(bf16[4,2304,2,128]{1,3,2,0:T(8,128)(2,1)} %collective-permute-done.23, bf16[6912,1728]{0,1:T(8,128)(2,1)} %param.6, bf16[4,2,1728,2,128]{4,2,3,1,0:T(8,128)(2,1)} %bitcast.138, s32[]{:T(128)S(6)} %select_n.80), kind=kOutput, calls=%fused_computation.5 | convolution fusion | flops 8160804864 | bytes 20938756 | tf_op jit(solution)/shard_map/vu,zuyx->zvyx/dot_general | solution.py:93
  182.0 20.1 %collective-permute-done.13 = bf16[2304,2,128]{0,2,1:T(8,128)(2,1)} collective-permute-done((bf16[2304,2,128]{0,2,1:T(8,128)(2,1)S(1)}, bf16[2304,2,128]{0,2,1:T(8,128)(2,1)}, u32[]{:S(2)}, u32[]{:S(2)}) %collective-permute-start.13) | collective-permute-done | bytes 1179680 | tf_op jit(solution)/shard_map/ppermute | solution.py:21
  205.6 21.7 %collective-permute-done.24 = bf16[2304,2,128]{0,2,1:T(8,128)(2,1)S(1)} collective-permute-done((bf16[2304,2,128]{0,2,1:T(8,128)(2,1)S(1)}, bf16[2304,2,128]{0,2,1:T(8,128)(2,1)S(1)}, u32[]{:S(2)}, u32[]{:S(2)}) %collective-permute-start.24) | collective-permute-done | bytes 1179680 | tf_op jit(solution)/shard_map/ppermute | solution.py:21
  231.5 21.1 %collective-permute-done.3 = bf16[2304,2,128]{0,2,1:T(8,128)(2,1)S(1)} collective-permute-done((bf16[2304,2,128]{0,2,1:T(8,128)(2,1)S(1)}, bf16[2304,2,128]{0,2,1:T(8,128)(2,1)S(1)}, u32[]{:S(2)}, u32[]{:S(2)}) %collective-permute-start.3) | collective-permute-done | bytes 1179680 | tf_op jit(solution)/shard_map/ppermute | solution.py:21
  255.8 4.8 collective-permute-start.4
  260.6 17.3 %collective-permute-done.14 = bf16[2304,2,128]{0,2,1:T(8,128)(2,1)S(1)} collective-permute-done((bf16[2304,2,128]{0,2,1:T(8,128)(2,1)S(1)}, bf16[2304,2,128]{0,2,1:T(8,128)(2,1)S(1)}, u32[]{:S(2)}, u32[]{:S(2)}) %collective-permute-start.14) | collective-permute-done | bytes 1179680 | tf_op jit(solution)/shard_map/ppermute | solution.py:21
  281.0 4.6 collective-permute-start.15
  285.6 17.5 %collective-permute-done.25 = bf16[2304,2,128]{0,2,1:T(8,128)(2,1)S(1)} collective-permute-done((bf16[2304,2,128]{0,2,1:T(8,128)(2,1)S(1)}, bf16[2304,2,128]{0,2,1:T(8,128)(2,1)S(1)}, u32[]{:S(2)}, u32[]{:S(2)}) %collective-permute-start.25) | collective-permute-done | bytes 1179680 | tf_op jit(solution)/shard_map/ppermute | solution.py:21
  312.2 23.0 %collective-permute-done.28 = bf16[2304,2,128]{0,2,1:T(8,128)(2,1)S(1)} collective-permute-done((bf16[2304,2,128]{0,2,1:T(8,128)(2,1)S(1)}, bf16[2304,2,128]{0,2,1:T(8,128)(2,1)S(1)}, u32[]{:S(2)}, u32[]{:S(2)}) %collective-permute-start.28) | collective-permute-done | bytes 1179680 | tf_op jit(solution)/shard_map/ppermute | solution.py:21
  339.4 21.1 %collective-permute-done.7 = bf16[2304,2,128]{0,2,1:T(8,128)(2,1)S(1)} collective-permute-done((bf16[2304,2,128]{0,2,1:T(8,128)(2,1)S(1)}, bf16[2304,2,128]{0,2,1:T(8,128)(2,1)S(1)}, u32[]{:S(2)}, u32[]{:S(2)}) %collective-permute-start.7) | collective-permute-done | bytes 1179680 | tf_op jit(solution)/shard_map/ppermute | solution.py:21
  366.9 18.9 %collective-permute-done.18 = bf16[2304,2,128]{0,2,1:T(8,128)(2,1)S(1)} collective-permute-done((bf16[2304,2,128]{0,2,1:T(8,128)(2,1)S(1)}, bf16[2304,2,128]{0,2,1:T(8,128)(2,1)S(1)}, u32[]{:S(2)}, u32[]{:S(2)}) %collective-permute-start.18) | collective-permute-done | bytes 1179680 | tf_op jit(solution)/shard_map/ppermute | solution.py:21
  392.1 17.8 %collective-permute-done.29 = bf16[2304,2,128]{0,2,1:T(8,128)(2,1)S(1)} collective-permute-done((bf16[2304,2,128]{0,2,1:T(8,128)(2,1)S(1)}, bf16[2304,2,128]{0,2,1:T(8,128)(2,1)S(1)}, u32[]{:S(2)}, u32[]{:S(2)}) %collective-permute-start.29) | collective-permute-done | bytes 1179680 | tf_op jit(solution)/shard_map/ppermute | solution.py:21
  413.9 11.9 %collective-permute-done.9 = bf16[2304,1,128]{0,2,1:T(8,128)(2,1)S(1)} collective-permute-done((bf16[2304,1,128]{0,2,1:T(8,128)(2,1)S(1)}, bf16[2304,1,128]{0,2,1:T(8,128)(2,1)S(1)}, u32[]{:S(2)}, u32[]{:S(2)}) %collective-permute-start.9) | collective-permute-done | bytes 589856 | tf_op jit(solution)/shard_map/ppermute | solution.py:17
  427.4 10.7 %collective-permute-done.19 = bf16[2304,1,128]{0,2,1:T(8,128)(2,1)S(1)} collective-permute-done((bf16[2304,1,128]{0,2,1:T(8,128)(2,1)S(1)}, bf16[2304,1,128]{0,2,1:T(8,128)(2,1)S(1)}, u32[]{:S(2)}, u32[]{:S(2)}) %collective-permute-start.19) | collective-permute-done | bytes 589856 | tf_op jit(solution)/shard_map/ppermute | solution.py:12
  447.2 12.5 %collective-permute-done.20 = bf16[2304,1,128]{0,2,1:T(8,128)(2,1)S(1)} collective-permute-done((bf16[2304,1,128]{0,2,1:T(8,128)(2,1)S(1)}, bf16[2304,1,128]{0,2,1:T(8,128)(2,1)S(1)}, u32[]{:S(2)}, u32[]{:S(2)}) %collective-permute-start.20) | collective-permute-done | bytes 589856 | tf_op jit(solution)/shard_map/ppermute | solution.py:17
  464.7 7.3 %collective-permute-done.30 = bf16[2304,1,128]{0,2,1:T(8,128)(2,1)S(1)} collective-permute-done((bf16[2304,1,128]{0,2,1:T(8,128)(2,1)S(1)}, bf16[2304,1,128]{0,2,1:T(8,128)(2,1)S(1)}, u32[]{:S(2)}, u32[]{:S(2)}) %collective-permute-start.30) | collective-permute-done | bytes 589856 | tf_op jit(solution)/shard_map/ppermute | solution.py:12
  478.6 6.5 %copy.10 = bf16[1,6912,2,128]{3,2,1,0:T(2,128)(2,1)} copy(bf16[1,6912,2,128]{1,3,2,0:T(8,128)(2,1)S(1)} %maximum_bitcast_fusion) | data formatting | bytes 7077888 | tf_op jit(solution)/shard_map/broadcast_in_dim | solution.py:108
  (92 shorter events, 79.7 us)
Async XLA Ops:
  2.5 78.4 %collective-permute-start = (bf16[4,1728,2,128]{3,1,2,0:T(8,128)(2,1)S(1)}, bf16[4,1728,2,128]{3,1,2,0:T(8,128)(2,1)}, u32[]{:S(2)}, u32[]{:S(2)}) collective-permute-start(bf16[4,1728,2,128]{3,1,2,0:T(8,128)(2,1)S(1)} %copy.8), channel_id=1, source_target_pairs={{0,2},{2,0},{1,3},{3,1},{4,6},{6,4},{5,7},{7,5},{8,10},{10,8},{9,1... | collective-permute-start | bytes 10616840 | tf_op jit(solution)/shard_map/ppermute | solution.py:77
  131.6 34.3 %collective-permute-start.23 = (bf16[4,2304,2,128]{1,3,2,0:T(8,128)(2,1)}, bf16[4,2304,2,128]{1,3,2,0:T(8,128)(2,1)}, u32[]{:S(2)}, u32[]{:S(2)}) collective-permute-start(bf16[4,2304,2,128]{1,3,2,0:T(8,128)(2,1)} %fusion.39), channel_id=1, source_target_pairs={{0,4},{4,0},{8,12},{12,8},{16,20},{20,16},{24,28},{28,24},{1,5},{5... | collective-permute-start | bytes 14155784 | tf_op jit(solution)/shard_map/ppermute | solution.py:21
  146.1 34.9 %collective-permute-start.2 = (bf16[2304,2,128]{0,2,1:T(8,128)(2,1)S(1)}, bf16[2304,2,128]{0,2,1:T(8,128)(2,1)S(1)}, u32[]{:S(2)}, u32[]{:S(2)}) collective-permute-start(bf16[2304,2,128]{0,2,1:T(8,128)(2,1)S(1)} %get-tuple-element.25), channel_id=1, source_target_pairs={{0,8},{4,12},{1,9},{5,13},{2,10},{6,14},{3,11},{7,15}} | collective-permute-start | bytes 3538952 | tf_op jit(solution)/shard_map/ppermute | solution.py:21
  147.4 82.2 %collective-permute-start.5 = (bf16[2304,2,128]{0,2,1:T(8,128)(2,1)S(1)}, bf16[2304,2,128]{0,2,1:T(8,128)(2,1)}, u32[]{:S(2)}, u32[]{:S(2)}) collective-permute-start(bf16[2304,2,128]{0,2,1:T(8,128)(2,1)S(1)} %get-tuple-element.26), channel_id=1, source_target_pairs={{24,16},{28,20},{25,17},{29,21},{26,18},{30,22},{27,19},{31,23}} | collective-permute-start | bytes 3538952 | tf_op jit(solution)/shard_map/ppermute | solution.py:21
  162.9 39.2 %collective-permute-start.13 = (bf16[2304,2,128]{0,2,1:T(8,128)(2,1)S(1)}, bf16[2304,2,128]{0,2,1:T(8,128)(2,1)}, u32[]{:S(2)}, u32[]{:S(2)}) collective-permute-start(bf16[2304,2,128]{0,2,1:T(8,128)(2,1)S(1)} %get-tuple-element.29), channel_id=1, source_target_pairs={{0,8},{4,12},{1,9},{5,13},{2,10},{6,14},{3,11},{7,15}} | collective-permute-start | bytes 3538952 | tf_op jit(solution)/shard_map/ppermute | solution.py:21
  164.2 91.5 %collective-permute-start.16 = (bf16[2304,2,128]{0,2,1:T(8,128)(2,1)S(1)}, bf16[2304,2,128]{0,2,1:T(8,128)(2,1)}, u32[]{:S(2)}, u32[]{:S(2)}) collective-permute-start(bf16[2304,2,128]{0,2,1:T(8,128)(2,1)S(1)} %get-tuple-element.30), channel_id=1, source_target_pairs={{24,16},{28,20},{25,17},{29,21},{26,18},{30,22},{27,19},{31,23}} | collective-permute-start | bytes 3538952 | tf_op jit(solution)/shard_map/ppermute | solution.py:21
  179.7 47.6 %collective-permute-start.24 = (bf16[2304,2,128]{0,2,1:T(8,128)(2,1)S(1)}, bf16[2304,2,128]{0,2,1:T(8,128)(2,1)S(1)}, u32[]{:S(2)}, u32[]{:S(2)}) collective-permute-start(bf16[2304,2,128]{0,2,1:T(8,128)(2,1)S(1)} %get-tuple-element.33), channel_id=1, source_target_pairs={{0,8},{4,12},{1,9},{5,13},{2,10},{6,14},{3,11},{7,15}} | collective-permute-start | bytes 3538952 | tf_op jit(solution)/shard_map/ppermute | solution.py:21
  181.0 100.0 %collective-permute-start.27 = (bf16[2304,2,128]{0,2,1:T(8,128)(2,1)S(1)}, bf16[2304,2,128]{0,2,1:T(8,128)(2,1)S(1)}, u32[]{:S(2)}, u32[]{:S(2)}) collective-permute-start(bf16[2304,2,128]{0,2,1:T(8,128)(2,1)S(1)} %get-tuple-element.34), channel_id=1, source_target_pairs={{24,16},{28,20},{25,17},{29,21},{26,18},{30,22},{27,19},{31,23}} | collective-permute-start | bytes 3538952 | tf_op jit(solution)/shard_map/ppermute | solution.py:21
  202.1 50.5 %collective-permute-start.3 = (bf16[2304,2,128]{0,2,1:T(8,128)(2,1)S(1)}, bf16[2304,2,128]{0,2,1:T(8,128)(2,1)S(1)}, u32[]{:S(2)}, u32[]{:S(2)}) collective-permute-start(bf16[2304,2,128]{0,2,1:T(8,128)(2,1)S(1)} %fusion.95), channel_id=1, source_target_pairs={{0,8},{4,12},{8,16},{12,20},{1,9},{5,13},{9,17},{13,21},{2,10},{6,... | collective-permute-start | bytes 3538952 | tf_op jit(solution)/shard_map/ppermute | solution.py:21
  227.3 50.6 %collective-permute-start.14 = (bf16[2304,2,128]{0,2,1:T(8,128)(2,1)S(1)}, bf16[2304,2,128]{0,2,1:T(8,128)(2,1)S(1)}, u32[]{:S(2)}, u32[]{:S(2)}) collective-permute-start(bf16[2304,2,128]{0,2,1:T(8,128)(2,1)S(1)} %fusion.89), channel_id=1, source_target_pairs={{0,8},{4,12},{8,16},{12,20},{1,9},{5,13},{9,17},{13,21},{2,10},{6,... | collective-permute-start | bytes 3538952 | tf_op jit(solution)/shard_map/ppermute | solution.py:21
  229.5 73.6 %collective-permute-start.25 = (bf16[2304,2,128]{0,2,1:T(8,128)(2,1)S(1)}, bf16[2304,2,128]{0,2,1:T(8,128)(2,1)S(1)}, u32[]{:S(2)}, u32[]{:S(2)}) collective-permute-start(bf16[2304,2,128]{0,2,1:T(8,128)(2,1)S(1)} %fusion.83), channel_id=1, source_target_pairs={{0,8},{4,12},{8,16},{12,20},{1,9},{5,13},{9,17},{13,21},{2,10},{6,... | collective-permute-start | bytes 3538952 | tf_op jit(solution)/shard_map/ppermute | solution.py:21
  254.5 50.5 %collective-permute-start.6 = (bf16[2304,2,128]{0,2,1:T(8,128)(2,1)S(1)}, bf16[2304,2,128]{0,2,1:T(8,128)(2,1)S(1)}, u32[]{:S(2)}, u32[]{:S(2)}) collective-permute-start(bf16[2304,2,128]{0,2,1:T(8,128)(2,1)S(1)} %get-tuple-element.24), channel_id=1, source_target_pairs={{24,16},{28,20},{16,8},{20,12},{25,17},{29,21},{17,9},{21,13},{26,... | collective-permute-start | bytes 3538952 | tf_op jit(solution)/shard_map/ppermute | solution.py:21
  255.8 81.7 %collective-permute-start.4 = (bf16[2304,2,128]{0,2,1:T(8,128)(2,1)S(1)}, bf16[2304,2,128]{0,2,1:T(8,128)(2,1)S(1)}, u32[]{:S(2)}, u32[]{:S(2)}) collective-permute-start(bf16[2304,2,128]{0,2,1:T(8,128)(2,1)S(1)} %get-tuple-element.23), channel_id=1, source_target_pairs={{0,8},{4,12},{8,16},{12,20},{16,24},{20,28},{1,9},{5,13},{9,17},{1... | collective-permute-start | bytes 3538952 | tf_op jit(solution)/shard_map/ppermute | solution.py:21
  281.0 82.2 %collective-permute-start.15 = (bf16[2304,2,128]{0,2,1:T(8,128)(2,1)S(1)}, bf16[2304,2,128]{0,2,1:T(8,128)(2,1)S(1)}, u32[]{:S(2)}, u32[]{:S(2)}) collective-permute-start(bf16[2304,2,128]{0,2,1:T(8,128)(2,1)S(1)} %get-tuple-element.27), channel_id=1, source_target_pairs={{0,8},{4,12},{8,16},{12,20},{16,24},{20,28},{1,9},{5,13},{9,17},{1... | collective-permute-start | bytes 3538952 | tf_op jit(solution)/shard_map/ppermute | solution.py:21
  305.0 83.6 %collective-permute-start.26 = (bf16[2304,2,128]{0,2,1:T(8,128)(2,1)S(1)}, bf16[2304,2,128]{0,2,1:T(8,128)(2,1)S(1)}, u32[]{:S(2)}, u32[]{:S(2)}) collective-permute-start(bf16[2304,2,128]{0,2,1:T(8,128)(2,1)S(1)} %get-tuple-element.31), channel_id=1, source_target_pairs={{0,8},{4,12},{8,16},{12,20},{16,24},{20,28},{1,9},{5,13},{9,17},{1... | collective-permute-start | bytes 3538952 | tf_op jit(solution)/shard_map/ppermute | solution.py:21
  310.0 50.6 %collective-permute-start.7 = (bf16[2304,2,128]{0,2,1:T(8,128)(2,1)S(1)}, bf16[2304,2,128]{0,2,1:T(8,128)(2,1)S(1)}, u32[]{:S(2)}, u32[]{:S(2)}) collective-permute-start(bf16[2304,2,128]{0,2,1:T(8,128)(2,1)S(1)} %fusion.94), channel_id=1, source_target_pairs={{24,16},{28,20},{16,8},{20,12},{8,0},{12,4},{25,17},{29,21},{17,9}... | collective-permute-start | bytes 3538952 | tf_op jit(solution)/shard_map/ppermute | solution.py:21
  335.3 50.6 %collective-permute-start.18 = (bf16[2304,2,128]{0,2,1:T(8,128)(2,1)S(1)}, bf16[2304,2,128]{0,2,1:T(8,128)(2,1)S(1)}, u32[]{:S(2)}, u32[]{:S(2)}) collective-permute-start(bf16[2304,2,128]{0,2,1:T(8,128)(2,1)S(1)} %fusion.88), channel_id=1, source_target_pairs={{24,16},{28,20},{16,8},{20,12},{8,0},{12,4},{25,17},{29,21},{17,9}... | collective-permute-start | bytes 3538952 | tf_op jit(solution)/shard_map/ppermute | solution.py:21
  337.5 72.4 %collective-permute-start.29 = (bf16[2304,2,128]{0,2,1:T(8,128)(2,1)S(1)}, bf16[2304,2,128]{0,2,1:T(8,128)(2,1)S(1)}, u32[]{:S(2)}, u32[]{:S(2)}) collective-permute-start(bf16[2304,2,128]{0,2,1:T(8,128)(2,1)S(1)} %fusion.82), channel_id=1, source_target_pairs={{24,16},{28,20},{16,8},{20,12},{8,0},{12,4},{25,17},{29,21},{17,9}... | collective-permute-start | bytes 3538952 | tf_op jit(solution)/shard_map/ppermute | solution.py:21
  361.0 79.0 %collective-permute-start.10 = (bf16[2304,2,128]{0,2,1:T(8,128)(2,1)S(1)}, bf16[2304,2,128]{0,2,1:T(8,128)(2,1)S(1)}, u32[]{:S(2)}, u32[]{:S(2)}) collective-permute-start(bf16[2304,2,128]{0,2,1:T(8,128)(2,1)S(1)} %fusion.98), channel_id=1, source_target_pairs={{0,4},{4,8},{8,12},{12,16},{16,20},{20,24},{24,28},{1,5},{5,9},{9,... | collective-permute-start | bytes 3538952 | tf_op jit(solution)/shard_map/ppermute | solution.py:12
  363.3 80.4 %collective-permute-start.11 = (bf16[2304,2,128]{0,2,1:T(8,128)(2,1)S(1)}, bf16[2304,2,128]{0,2,1:T(8,128)(2,1)S(1)}, u32[]{:S(2)}, u32[]{:S(2)}) collective-permute-start(bf16[2304,2,128]{0,2,1:T(8,128)(2,1)S(1)} %fusion.98), channel_id=1, source_target_pairs={{4,0},{8,4},{12,8},{16,12},{20,16},{24,20},{28,24},{5,1},{9,5},{13... | collective-permute-start | bytes 3538952 | tf_op jit(solution)/shard_map/ppermute | solution.py:17
  386.3 74.9 %collective-permute-start.21 = (bf16[2304,2,128]{0,2,1:T(8,128)(2,1)S(1)}, bf16[2304,2,128]{0,2,1:T(8,128)(2,1)S(1)}, u32[]{:S(2)}, u32[]{:S(2)}) collective-permute-start(bf16[2304,2,128]{0,2,1:T(8,128)(2,1)S(1)} %fusion.92), channel_id=1, source_target_pairs={{0,4},{4,8},{8,12},{12,16},{16,20},{20,24},{24,28},{1,5},{5,9},{9,... | collective-permute-start | bytes 3538952 | tf_op jit(solution)/shard_map/ppermute | solution.py:12
  412.0 50.5 %collective-permute-start.22 = (bf16[2304,2,128]{0,2,1:T(8,128)(2,1)S(1)}, bf16[2304,2,128]{0,2,1:T(8,128)(2,1)S(1)}, u32[]{:S(2)}, u32[]{:S(2)}) collective-permute-start(bf16[2304,2,128]{0,2,1:T(8,128)(2,1)S(1)} %fusion.92), channel_id=1, source_target_pairs={{4,0},{8,4},{12,8},{16,12},{20,16},{24,20},{28,24},{5,1},{9,5},{13... | collective-permute-start | bytes 3538952 | tf_op jit(solution)/shard_map/ppermute | solution.py:17
  438.1 38.1 %collective-permute-start.32 = (bf16[2304,2,128]{0,2,1:T(8,128)(2,1)S(1)}, bf16[2304,2,128]{0,2,1:T(8,128)(2,1)S(1)}, u32[]{:S(2)}, u32[]{:S(2)}) collective-permute-start(bf16[2304,2,128]{0,2,1:T(8,128)(2,1)S(1)} %fusion.86), channel_id=1, source_target_pairs={{0,4},{4,8},{8,12},{12,16},{16,20},{20,24},{24,28},{1,5},{5,9},{9,... | collective-permute-start | bytes 3538952 | tf_op jit(solution)/shard_map/ppermute | solution.py:12
  440.0 36.1 %collective-permute-start.33 = (bf16[2304,2,128]{0,2,1:T(8,128)(2,1)S(1)}, bf16[2304,2,128]{0,2,1:T(8,128)(2,1)S(1)}, u32[]{:S(2)}, u32[]{:S(2)}) collective-permute-start(bf16[2304,2,128]{0,2,1:T(8,128)(2,1)S(1)} %fusion.86), channel_id=1, source_target_pairs={{4,0},{8,4},{12,8},{16,12},{20,16},{24,20},{28,24},{5,1},{9,5},{13... | collective-permute-start | bytes 3538952 | tf_op jit(solution)/shard_map/ppermute | solution.py:17
  (14 other events, 293.4 us)
